TPU v7x, 32 devices: a whole 2x2x4 slice. The times are simulated.
32 devices in a mesh: grp: 2 (over x), tm: 16 (over z, y, core).
Axes of the slice: x: 2, y: 2, z: 4, core: 2. Of those that a mesh axis runs over, the one named last changes fastest.
Arguments:
- states: float32 [32, 84, 12, 128], P(('grp', 'tm')), parts along dimension 0, may hold values from -6 to 6
- slab_steps: int32 [32], P(('grp', 'tm')), parts along dimension 0, may hold values from 0 to 999
- offset: int32 [2], P('grp'), parts along dimension 0, may hold values from 0 to 999
- log_sigma: float32 [1000], replicated, may hold values from -2 to 2
- step_size: float32 [1000], replicated, may hold values from -0.12 to -0.03
- w_in: bfloat16 [9, 256, 84], replicated, may hold values from -0.21875 to 0.21875
- w_mid: bfloat16 [9, 256, 256], replicated, may hold values from -0.125 to 0.125
- w_out: bfloat16 [9, 84, 256], replicated, may hold values from -0.125 to 0.125
- embed: float32 [256], replicated, may hold values from -5 to 5
Outputs:
- new_states: float32 [32, 84, 12, 128], P(('grp', 'tm')), parts along dimension 0
There are 2 independent parts, one for each index of `grp`. A program takes and returns all parts, laid end to end along the dimension named above; an argument that names none is the same for every part. Nothing has to cross between parts.
All inputs are finite; a program needn't handle non-finite values.
Results may differ from a plain program's by a relative error of at most 0.0011.
Values sent between devices are 32-bit elements; how exact they have to be, the bound alone decides.
A program may use at most 64 MiB of HBM per device.

v0:
```python
import jax
import jax.numpy as jnp
from jax import lax
from jax.sharding import PartitionSpec as P

TABLE = 1000
SWEEPS = 2


def convolve(field, weights):
    channels, rows, cols = field.shape
    padded = jnp.pad(field, ((0, 0), (1, 1), (1, 1)))
    total = jnp.zeros((weights.shape[1], rows * cols), jnp.float32)
    for kernel_tap in range(9):
        row_shift = kernel_tap // 3
        col_shift = kernel_tap % 3
        window = padded[:, row_shift : row_shift + rows, col_shift : col_shift + cols].reshape(
            channels, rows * cols
        )
        total = total + jnp.dot(weights[kernel_tap], window, preferred_element_type=jnp.float32)
    return total


def drift_field(field, log_noise, w_in, w_mid, w_out, embed):
    fields, rows, cols = field.shape
    hidden = w_in.shape[1]
    first = convolve(field.astype(jnp.bfloat16), w_in) + log_noise * embed[:, None]
    first = jax.nn.silu(first).astype(jnp.bfloat16).reshape(hidden, rows, cols)
    second = jax.nn.silu(convolve(first, w_mid)).astype(jnp.bfloat16).reshape(hidden, rows, cols)
    return convolve(second, w_out).reshape(fields, rows, cols)


def earlier_sum(increment):
    owners = lax.axis_size("tm")
    flat = increment.reshape(1, -1)
    by_cells = lax.all_to_all(flat, "tm", split_axis=1, concat_axis=0, tiled=True)
    slab_ids = jnp.arange(owners, dtype=jnp.int32)
    lower = (slab_ids[:, None] > slab_ids[None, :]).astype(jnp.float32)
    exclusive = jnp.dot(
        lower, by_cells, precision=lax.Precision.HIGHEST, preferred_element_type=jnp.float32
    )
    back = lax.all_to_all(exclusive, "tm", split_axis=0, concat_axis=1, tiled=True)
    return back.reshape(increment.shape)


def shards(states, slab_steps, offset, log_sigma, step_size, w_in, w_mid, w_out, embed):
    owner = lax.axis_index("tm")
    table_row = (slab_steps[0] + offset[0]) % TABLE
    onehot = jnp.arange(TABLE, dtype=jnp.int32) == table_row
    log_noise = jnp.sum(jnp.where(onehot, log_sigma, 0.0))
    step_len = jnp.sum(jnp.where(onehot, step_size, 0.0))
    field = states[0]
    is_first = owner == 0
    before = field
    increment = field
    for sweep_index in range(SWEEPS):
        increment = step_len * drift_field(field, log_noise, w_in, w_mid, w_out, embed)
        increment = increment + jnp.where(is_first, field, jnp.zeros_like(field))
        before = earlier_sum(increment)
        if sweep_index + 1 < SWEEPS:
            field = jnp.where(is_first, field, before)
    result = before + increment
    return result[None]


def solution(mesh):
    in_specs = (
        P(("grp", "tm"), None, None, None),
        P(("grp", "tm")),
        P("grp"),
        P(),
        P(),
        P(),
        P(),
        P(),
        P(),
    )
    out_specs = P(("grp", "tm"), None, None, None)
    return jax.shard_map(shards, mesh=mesh, in_specs=in_specs, out_specs=out_specs, check_vma=False)
```

profile of v0, /device:TPU:0, one launch (start us, length us, event | category | flops | bytes accessed | tf_op | source)
XLA Modules:
  0.0 143.9 jit_solution(4096677743401641618)
XLA Ops:
  1.3 1.1 copy.120
  2.4 2.4 %convert_reduce_fusion = bf16[84,12,128]{2,1,0:T(8,128)(2,1)S(1)} fusion(f32[1,84,12,128]{3,0,2,1:T(1,128)} %param.9), kind=kLoop, calls=%fused_computation.130 | loop fusion | flops 129024 | bytes 774144 | tf_op jit(solution)/shard_map/convert_element_type | solution.py:27
  4.9 0.8 copy.88
  6.4 0.8 copy.87
  7.3 0.8 copy.85
  8.2 0.8 copy.86
  11.5 1.6 %convolution_bitcast_fusion.3 = f32[256,1536]{0,1:T(8,128)} fusion(bf16[84,1536]{1,0:T(8,128)(2,1)S(1)} %bitcast.384, bf16[9,256,84]{1,2,0:T(8,128)(2,1)S(1)} %copy-done.7), kind=kOutput, calls=%fused_computation.41 | convolution fusion | flops 66060288 | bytes 1888256 | tf_op jit(solution)/shard_map/dot_general | solution.py:20
  13.1 1.6 %convolution_bitcast_fusion.4 = f32[256,1536]{0,1:T(8,128)} fusion(bf16[84,1536]{1,0:T(8,128)(2,1)S(1)} %bitcast.382, bf16[9,256,84]{1,2,0:T(8,128)(2,1)S(1)} %copy-done.7), kind=kOutput, calls=%fused_computation.42 | convolution fusion | flops 66060288 | bytes 1888256 | tf_op jit(solution)/shard_map/dot_general | solution.py:20
  14.6 1.5 %convolution_bitcast_fusion.5 = f32[256,1536]{0,1:T(8,128)} fusion(bf16[84,1536]{1,0:T(8,128)(2,1)S(1)} %bitcast.381, bf16[9,256,84]{1,2,0:T(8,128)(2,1)S(1)} %copy-done.7), kind=kOutput, calls=%fused_computation.43 | convolution fusion | flops 66060288 | bytes 1888256 | tf_op jit(solution)/shard_map/dot_general | solution.py:20
  16.2 1.3 select_reduce_fusion
  17.5 1.3 broadcast_multiply_fusion
  18.8 1.4 convolution_add_fusion.27
  21.7 1.0 copy-done.4
  23.2 1.0 multiply_convert_fusion.3
  24.1 2.3 %pad_slice_fusion.40 = (bf16[256,12,128]{0,2,1:T(8,128)(2,1)S(1)}, bf16[256,12,128]{0,2,1:T(8,128)(2,1)S(1)}, bf16[256,12,128]{0,2,1:T(8,128)(2,1)S(1)}, bf16[25...) fusion(bf16[256,12,128]{0,2,1:T(8,128)(2,1)S(1)} %bitcast.349), kind=kLoop, calls=%fused_computation.111 | loop fusion | bytes 7077888 | tf_op jit(solution)/shard_map/slice | solution.py:17
  30.4 2.1 %pad_slice_fusion.32 = (bf16[256,12,128]{0,2,1:T(8,128)(2,1)S(1)}, bf16[256,12,128]{0,2,1:T(8,128)(2,1)S(1)}, bf16[256,12,128]{0,2,1:T(8,128)(2,1)S(1)}, bf16[25...) fusion(bf16[256,12,128]{0,2,1:T(8,128)(2,1)S(1)} %bitcast.333), kind=kLoop, calls=%fused_computation.103 | loop fusion | bytes 7077888 | tf_op jit(solution)/shard_map/slice | solution.py:17
  35.5 1.0 fusion.12
  37.8 21.4 %all_to_all.52 = f32[1,16,8064]{2,0,1:T(1,128)S(1)} all-to-all(f32[1,16,8064]{2,0,1:T(1,128)S(1)} %fusion.15), channel_id=1, replica_groups=mesh['grp'=2,'tm'=16] {'tm'}, dimensions={1} | all-to-all | bytes 1032192 | tf_op jit(solution)/shard_map/all_to_all | solution.py:36
  60.1 18.2 %all_to_all.53 = f32[16,1,8064]{2,1,0:T(1,128)S(1)} all-to-all(f32[16,1,8064]{2,1,0:T(1,128)S(1)} %copy.67), channel_id=1, replica_groups=mesh['grp'=2,'tm'=16] {'tm'}, dimensions={0} | all-to-all | bytes 1032192 | tf_op jit(solution)/shard_map/all_to_all | solution.py:42
  78.3 1.3 reduce.1
  79.5 1.0 reshape.322
  80.7 1.1 fusion.14
  88.8 2.1 %pad_slice_fusion.24 = (bf16[256,12,128]{0,2,1:T(8,128)(2,1)S(1)}, bf16[256,12,128]{0,2,1:T(8,128)(2,1)S(1)}, bf16[256,12,128]{0,2,1:T(8,128)(2,1)S(1)}, bf16[25...) fusion(bf16[256,12,128]{0,2,1:T(8,128)(2,1)S(1)} %bitcast.350), kind=kLoop, calls=%fused_computation.95 | loop fusion | bytes 7077888 | tf_op jit(solution)/shard_map/slice | solution.py:17
  94.9 2.4 %pad_slice_fusion.16 = (bf16[256,12,128]{0,2,1:T(8,128)(2,1)S(1)}, bf16[256,12,128]{0,2,1:T(8,128)(2,1)S(1)}, bf16[256,12,128]{0,2,1:T(8,128)(2,1)S(1)}, bf16[25...) fusion(bf16[256,12,128]{0,2,1:T(8,128)(2,1)S(1)} %bitcast.335), kind=kLoop, calls=%fused_computation.87 | loop fusion | bytes 7077888 | tf_op jit(solution)/shard_map/slice | solution.py:17
  100.3 0.9 fusion.13
  101.9 0.9 fusion.16
  102.8 18.2 %all_to_all.54 = f32[1,16,8064]{2,0,1:T(1,128)S(1)} all-to-all(f32[1,16,8064]{2,0,1:T(1,128)S(1)} %fusion.16), channel_id=1, replica_groups=mesh['grp'=2,'tm'=16] {'tm'}, dimensions={1} | all-to-all | bytes 1032192 | tf_op jit(solution)/shard_map/all_to_all | solution.py:36
  121.3 1.3 copy.79
  122.7 4.2 %all-to-all-start.3 = ((f32[16,1,8064]{2,1,0:T(1,128)}), f32[16,1,8064]{2,1,0:T(1,128)S(1)}, u32[]{:S(2)}, u32[]{:S(2)}) async-start(f32[16,1,8064]{2,1,0:T(1,128)} %copy.79), calls=%async_computation.3 | async-start | bytes 1032192 | tf_op jit(solution)/shard_map/all_to_all | solution.py:42
  127.0 14.1 %all-to-all-done.3 = f32[16,1,8064]{2,1,0:T(1,128)S(1)} async-done(((f32[16,1,8064]{2,1,0:T(1,128)}), f32[16,1,8064]{2,1,0:T(1,128)S(1)}, u32[]{:S(2)}, u32[]{:S(2)}) %all-to-all-start.3) | async-done | bytes 516128 | tf_op jit(solution)/shard_map/all_to_all | solution.py:42
  141.0 1.3 reduce.3
  142.6 1.3 copy.80
  (133 shorter events, 29.4 us)
Async XLA Ops:
  9.7 1.0 copy-start.7
  13.1 3.1 %copy-start.12 = (f32[1000]{0:T(1024)S(1)}, f32[1000]{0:T(1024)}, u32[]{:S(2)}) copy-start(f32[1000]{0:T(1024)} %param.12) | copy-start | bytes 12004
  18.8 1.4 copy-start.10
  20.2 1.0 copy-start.9
  20.2 1.5 %copy-start.6 = (f32[256,1536]{0,1:T(8,128)S(1)}, f32[256,1536]{0,1:T(8,128)}, u32[]{:S(2)}) copy-start(f32[256,1536]{0,1:T(8,128)} %convolution_bitcast_fusion.5) | copy-start | bytes 4718596
  21.1 1.5 %copy-start.4 = (f32[256,1536]{0,1:T(8,128)S(1)}, f32[256,1536]{0,1:T(8,128)}, u32[]{:S(2)}) copy-start(f32[256,1536]{0,1:T(8,128)} %convolution_bitcast_fusion.3) | copy-start | bytes 4718596
  21.1 2.0 %copy-start.5 = (f32[256,1536]{0,1:T(8,128)S(1)}, f32[256,1536]{0,1:T(8,128)}, u32[]{:S(2)}) copy-start(f32[256,1536]{0,1:T(8,128)} %convolution_bitcast_fusion.4) | copy-start | bytes 4718596
  21.1 2.0 %copy-start.11 = (bf16[11,8,12,128]{3,1,2,0:T(8,128)(2,1)S(1)}, bf16[11,8,12,128]{3,1,2,0:T(8,128)(2,1)}, u32[]{:S(2)}) copy-start(bf16[11,8,12,128]{3,1,2,0:T(8,128)(2,1)} %copy.88) | copy-start | bytes 811012
  24.1 2.3 %copy-start.1 = (bf16[9,256,256]{2,1,0:T(8,128)(2,1)S(1)}, bf16[9,256,256]{2,1,0:T(8,128)(2,1)}, u32[]{:S(2)}) copy-start(bf16[9,256,256]{2,1,0:T(8,128)(2,1)} %param.15) | copy-start | bytes 3538948
  30.4 2.1 %copy-start.2 = (bf16[9,84,256]{2,1,0:T(8,128)(2,1)S(1)}, bf16[9,84,256]{2,1,0:T(8,128)(2,1)}, u32[]{:S(2)}) copy-start(bf16[9,84,256]{2,1,0:T(8,128)(2,1)} %param.16) | copy-start | bytes 1161220
  35.5 1.6 %copy-start = (f32[1,84,12,128]{3,0,2,1:T(1,128)S(1)}, f32[1,84,12,128]{3,0,2,1:T(1,128)}, u32[]{:S(2)}) copy-start(f32[1,84,12,128]{3,0,2,1:T(1,128)} %param.9) | copy-start | bytes 1548292
  83.9 1.0 copy-start.8
  94.9 2.4 %copy-start.3 = (bf16[9,84,256]{2,1,0:T(8,128)(2,1)S(1)}, bf16[9,84,256]{2,1,0:T(8,128)(2,1)}, u32[]{:S(2)}) copy-start(bf16[9,84,256]{2,1,0:T(8,128)(2,1)} %param.16) | copy-start | bytes 1161220
  122.7 18.4 %all-to-all-start.3 = ((f32[16,1,8064]{2,1,0:T(1,128)}), f32[16,1,8064]{2,1,0:T(1,128)S(1)}, u32[]{:S(2)}, u32[]{:S(2)}) async-start(f32[16,1,8064]{2,1,0:T(1,128)} %copy.79), calls=%async_computation.3 | async-start | bytes 1032192 | tf_op jit(solution)/shard_map/all_to_all | solution.py:42
where the time goes:
time: 145 us; the launch traced here: 144 us
  blocking collectives  57.7 us (40%)
  matrix products  28.8 us (20%)
  local copies, waits for them, and re-layouts  26.4 us (18%)
  waiting for transfers between devices  14.1 us (10%)
  other arithmetic  10.5 us (7%)
  starting transfers between devices  4.22 us (3%)
  between operations  2.25 us (2%)
    all_to_all x2, blocking collectives, earlier_sum(): lax.all_to_all(flat, 'tm', split_axis=1, concat_axis=0, tiled=True)  39.5 us
    dot_general x54, matrix products, convolve(): jnp.dot(weights[kernel_tap], window, preferred_element_type=jnp.float32)  28 us
    all_to_all x1, blocking collectives, earlier_sum(): lax.all_to_all(exclusive, 'tm', split_axis=0, concat_axis=1, tiled=True)  18.2 us
    all_to_all x1, waiting for transfers between devices, earlier_sum(): lax.all_to_all(exclusive, 'tm', split_axis=0, concat_axis=1, tiled=True)  14.1 us
    slice x22, local copies, waits for them, and re-layouts, convolve(): padded[:, row_shift:row_shift + rows, col_shift:col_shift + cols]  10.9 us
    unnamed x63, local copies, waits for them, and re-layouts  9.87 us
    all_to_all x1, starting transfers between devices, earlier_sum(): lax.all_to_all(exclusive, 'tm', split_axis=0, concat_axis=1, tiled=True)  4.22 us
    convert_element_type x2, other arithmetic, drift_field(): field.astype(jnp.bfloat16)  3.47 us
  transfers between devices with their start and end apart: 1, of which 1 were waited for; matrix products, arithmetic and copies ran while one was open for 0% of the time, Pallas kernels for 0%

commit v1 on v0

v1 whole, which is shorter than its diff:
```python
import functools

import jax
import jax.numpy as jnp
from jax import lax
from jax.experimental import pallas as pl
from jax.experimental.pallas import tpu as pltpu
from jax.sharding import PartitionSpec as P

SWEEPS = 2
MESH = pl.DeviceIdType.MESH


def up(value, multiple):
    return (value + multiple - 1) // multiple * multiple


def kernel(dims, x_hbm, steps_ref, offset_ref, ls_ref, ss_ref, win_hbm, wmid_hbm, wout_hbm, emb_ref, out_ref,
           win_v, wout_v, w1, w2, w3, eb, xf, xc, u1, u2, inc,
           ra, rp, rs, re, rr, sf, sb, se, sr,
           load_sem, wmid_sem, ssem, rsem):
    n, inner, F, CH, H, W, FP = dims
    outer = n // (2 * inner)
    K = H // 2
    me = lax.axis_index("tm")
    core = lax.rem(me, 2)
    chip = me // 2
    b = lax.rem(chip, inner)
    a = chip // inner
    partner = me + 1 - 2 * core
    b_next, b_prev = me + 2, me - 2
    a_next, a_prev = me + 2 * inner, me - 2 * inner

    loads = [
        pltpu.make_async_copy(x_hbm, xf.at[pl.ds(1, H)], load_sem.at[0]),
        pltpu.make_async_copy(win_hbm, win_v, load_sem.at[1]),
        pltpu.make_async_copy(wout_hbm, wout_v, load_sem.at[2]),
    ]
    for tap in range(9):
        ka, kb = tap // 3, tap % 3
        loads.append(
            pltpu.make_async_copy(
                wmid_hbm.at[tap], w2.at[pl.ds(kb * CH, CH), pl.ds(ka * CH, CH)], wmid_sem.at[tap]
            )
        )
    loads[1].start()
    loads[0].start()
    for copy in loads[2:]:
        copy.start()

    @pl.when(b == 0)
    def _():
        rp[...] = jnp.zeros_like(rp)

    @pl.when(b == inner - 1)
    def _():
        rs[...] = jnp.zeros_like(rs)

    @pl.when(a == 0)
    def _():
        re[...] = jnp.zeros_like(re)

    barrier = pltpu.get_barrier_semaphore()

    def greet(device):
        pl.semaphore_signal(barrier, inc=1, device_id={"tm": device}, device_id_type=MESH)

    greet(partner)
    for there, device in ((b > 0, b_prev), (b < inner - 1, b_next), (a > 0, a_prev), (a < outer - 1, a_next)):
        pl.when(there)(functools.partial(greet, device))

    table_row = lax.rem(steps_ref[0] + offset_ref[0], ls_ref.shape[0])
    log_noise = ls_ref[table_row]
    step_len = ss_ref[table_row]
    first = jnp.where(me == 0, 1.0, 0.0).astype(jnp.float32)

    for block in range(CH // 128):
        row = emb_ref[pl.ds(block, 1), :] * log_noise
        eb[pl.ds(block * 128, 128), :] = jnp.transpose(jnp.broadcast_to(row, (128, 128)))
    zero_row = jnp.zeros((CH, W), jnp.bfloat16)
    for edge in (0, H + 1):
        u1[edge] = zero_row
        u2[edge] = zero_row
        xf[edge] = jnp.zeros((F, W), jnp.float32)

    loads[1].wait()
    for kb in range(3):
        parts = [win_v[3 * ka + kb].astype(jnp.float32) for ka in range(3)]
        parts.append(jnp.zeros((CH, w1.shape[1] - 3 * F), jnp.float32))
        w1[pl.ds(kb * CH, CH), :] = jnp.concatenate(parts, axis=1).astype(jnp.bfloat16)
    loads[0].wait()

    lane = lax.broadcasted_iota(jnp.int32, (1, W), 1)

    def combine(product, rows, base, j):
        cols = slice(j * W, (j + 1) * W)
        left = pltpu.roll(product[0:rows, cols], 1, axis=1)
        mid = product[base:base + rows, cols]
        right = pltpu.roll(product[2 * base:2 * base + rows, cols], W - 1, axis=1)
        return mid + jnp.where(lane == 0, 0.0, left) + jnp.where(lane == W - 1, 0.0, right)

    def silu(value):
        half = 0.5 * value
        return half * (1.0 + jnp.tanh(half))

    def stage(r):
        parts = [xf[r], xf[r + 1], xf[r + 2], jnp.zeros((w1.shape[1] - 3 * F, W), jnp.float32)]
        xc[r] = jnp.concatenate(parts, axis=0).astype(jnp.bfloat16)

    def conv1(k):
        r = 2 * k
        stage(r)
        stage(r + 1)
        z = jnp.concatenate([xc[r], xc[r + 1]], axis=1)
        product = jnp.dot(w1[...], z, preferred_element_type=jnp.float32)
        for j in range(2):
            u1[r + j + 1] = silu(combine(product, CH, CH, j) + eb[...]).astype(jnp.bfloat16)

    def taps(u, r):
        return jnp.concatenate(
            [jnp.concatenate([u[r + ka], u[r + ka + 1]], axis=1) for ka in range(3)], axis=0
        )

    def conv2(k):
        r = 2 * k
        product = jnp.dot(w2[...], taps(u1, r), preferred_element_type=jnp.float32)
        for j in range(2):
            u2[r + j + 1] = silu(combine(product, CH, CH, j)).astype(jnp.bfloat16)

    def conv3(s, k):
        r = 2 * k
        product = jnp.dot(w3[...], taps(u2, r), preferred_element_type=jnp.float32)
        for j in range(2):
            inc[s, r + j] = step_len * combine(product, F, FP, j) + first * xf[r + j + 1]

    def remote(kind, s, k, src, dst, device):
        return pltpu.make_async_remote_copy(
            src_ref=src,
            dst_ref=dst,
            send_sem=ssem.at[kind, s, k],
            recv_sem=rsem.at[kind, s, k],
            device_id={"tm": device},
            device_id_type=MESH,
        )

    def own(k):
        return 2 * k + core

    def other(k):
        return 2 * k + 1 - core

    def pair(s, k):
        return remote(0, s, k, inc.at[s, other(k)], ra.at[s, k], partner)

    def forward(s, k):
        return remote(1, s, k, sf.at[s, k], rp.at[s, k], b_next)

    def backward(s, k):
        return remote(2, s, k, sb.at[s, k], rs.at[s, k], b_prev)

    def chain(s, k):
        return remote(3, s, k, se.at[s, k], re.at[s, k], a_next)

    def result(s, k):
        return remote(4, s, k, sr.at[s, k], rr.at[s, k], partner)

    def send_pair(s, k):
        pair(s, k).start()

    def send_chip(s, k):
        pair(s, k).wait_recv()
        chip_sum = inc[s, own(k)] + ra[s, k]
        sf[s, k] = chip_sum
        sb[s, k] = chip_sum

        @pl.when(b == 0)
        def _():
            forward(s, k).start()

        @pl.when(b == inner - 1)
        def _():
            backward(s, k).start()

    def send_plane(s, k):
        middle = (b > 0) & (b < inner - 1)
        chip_sum = inc[s, own(k)] + ra[s, k]

        @pl.when(b > 0)
        def _():
            forward(s, k).wait_recv()

        if inner > 2:
            @pl.when(middle)
            def _():
                sf[s, k] = rp[s, k] + chip_sum
                forward(s, k).start()

        @pl.when(b < inner - 1)
        def _():
            backward(s, k).wait_recv()

        if inner > 2:
            @pl.when(middle)
            def _():
                sb[s, k] = rs[s, k] + chip_sum
                backward(s, k).start()

        @pl.when(a > 0)
        def _():
            chain(s, k).wait_recv()

        before = re[s, k] + rp[s, k]

        @pl.when(a < outer - 1)
        def _():
            se[s, k] = before + chip_sum + rs[s, k]
            chain(s, k).start()

        is_second = core.astype(jnp.float32)
        sr[s, k] = before + (1.0 - is_second) * inc[s, own(k)]
        result(s, k).start()
        finish(s, own(k), before + is_second * ra[s, k])

    def finish(s, r, before):
        if s + 1 < SWEEPS:
            xf[r + 1] = before + first * xf[r + 1]
        else:
            out_ref[r] = before + inc[s, r]

    def receive(s, k):
        result(s, k).wait_recv()
        finish(s, other(k), rr[s, k])

    for s in range(SWEEPS):
        for t in range(K + 2):
            if t < K:
                conv1(t)
            if s == 0 and t == 0:
                for copy in loads[3:]:
                    copy.wait()
            if 1 <= t <= K:
                conv2(t - 1)
            if s == 0 and t == 1:
                loads[2].wait()
                for tap in range(9):
                    ka, kb = tap // 3, tap % 3
                    padded = jnp.concatenate(
                        [wout_v[tap].astype(jnp.float32), jnp.zeros((FP - F, CH), jnp.float32)], axis=0
                    )
                    w3[pl.ds(kb * FP, FP), pl.ds(ka * CH, CH)] = padded.astype(jnp.bfloat16)
                count = 1 + (b > 0).astype(jnp.int32) + (b < inner - 1).astype(jnp.int32)
                count = count + (a > 0).astype(jnp.int32) + (a < outer - 1).astype(jnp.int32)
                pl.semaphore_wait(barrier, count)
            if t >= 2:
                conv3(s, t - 2)
                send_pair(s, t - 2)
            if t >= 3:
                send_chip(s, t - 3)
            if t >= 4:
                send_plane(s, t - 4)
        send_chip(s, K - 1)
        send_plane(s, K - 2)
        send_plane(s, K - 1)
        for k in range(K):
            receive(s, k)

    for s in range(SWEEPS):
        for k in range(K):
            pair(s, k).wait_send()
            pl.when(b < inner - 1)(lambda s=s, k=k: forward(s, k).wait_send())
            pl.when(b > 0)(lambda s=s, k=k: backward(s, k).wait_send())
            pl.when(a < outer - 1)(lambda s=s, k=k: chain(s, k).wait_send())
            result(s, k).wait_send()


def shards(n, states, slab_steps, offset, log_sigma, step_size, w_in, w_mid, w_out, embed):
    _, F, H, W = states.shape
    CH = w_in.shape[1]
    chips = n // 2
    inner = 1
    while 4 * inner * inner <= chips:
        inner *= 2
    FP = up(F, 16)
    K1 = up(3 * F, 128)
    K = H // 2
    x = jnp.transpose(states[0], (1, 0, 2))
    vmem = pl.BlockSpec(memory_space=pltpu.VMEM)
    smem = pl.BlockSpec(memory_space=pltpu.SMEM)
    hbm = pl.BlockSpec(memory_space=pl.ANY)
    bf16, f32 = jnp.bfloat16, jnp.float32
    slot = pltpu.VMEM((SWEEPS, K, F, W), f32)
    flops = SWEEPS * 2 * 9 * (2 * F * CH + CH * CH) * H * W
    out = pl.pallas_call(
        functools.partial(kernel, (n, inner, F, CH, H, W, FP)),
        out_shape=jax.ShapeDtypeStruct((H, F, W), f32),
        in_specs=[hbm, smem, smem, smem, smem, hbm, hbm, hbm, vmem],
        out_specs=vmem,
        scratch_shapes=[
            pltpu.VMEM(w_in.shape, bf16),
            pltpu.VMEM(w_out.shape, bf16),
            pltpu.VMEM((3 * CH, K1), bf16),
            pltpu.VMEM((3 * CH, 3 * CH), bf16),
            pltpu.VMEM((3 * FP, 3 * CH), bf16),
            pltpu.VMEM((CH, W), f32),
            pltpu.VMEM((H + 2, F, W), f32),
            pltpu.VMEM((H, K1, W), bf16),
            pltpu.VMEM((H + 2, CH, W), bf16),
            pltpu.VMEM((H + 2, CH, W), bf16),
            pltpu.VMEM((SWEEPS, H, F, W), f32),
            slot, slot, slot, slot, slot, slot, slot, slot, slot,
            pltpu.SemaphoreType.DMA((3,)),
            pltpu.SemaphoreType.DMA((9,)),
            pltpu.SemaphoreType.DMA((5, SWEEPS, K)),
            pltpu.SemaphoreType.DMA((5, SWEEPS, K)),
        ],
        compiler_params=pltpu.CompilerParams(
            collective_id=0, has_side_effects=True, vmem_limit_bytes=40 * 1024 * 1024
        ),
        cost_estimate=pl.CostEstimate(
            flops=flops, bytes_accessed=4 * 1024 * 1024, transcendentals=SWEEPS * 2 * CH * H * W
        ),
    )(x, slab_steps, offset, log_sigma, step_size, w_in, w_mid, w_out, embed.reshape(CH // 128, 128))
    return jnp.transpose(out, (1, 0, 2))[None]


def solution(mesh):
    in_specs = (
        P(("grp", "tm"), None, None, None),
        P(("grp", "tm")),
        P("grp"),
        P(),
        P(),
        P(),
        P(),
        P(),
        P(),
    )
    out_specs = P(("grp", "tm"), None, None, None)
    body = functools.partial(shards, mesh.shape["tm"])
    return jax.shard_map(body, mesh=mesh, in_specs=in_specs, out_specs=out_specs, check_vma=False)
```

time: 145 us -> 50 us (0.34)
  the two profiles are of different devices: /device:TPU:0 before, /device:TPU:25 now
where the time goes in v1:
time: 50 us; the launch traced here: 49.6 us
  Pallas kernels  44.3 us (89%)
  local copies, waits for them, and re-layouts  3.77 us (8%)
  between operations  1.49 us (3%)
    pallas_call x1, Pallas kernels, shards(): pl.pallas_call(functools.partial(kernel, (n, inner, F, CH, H, W, FP)), ou...  44.3 us
    unnamed x12, local copies, waits for them, and re-layouts  2.45 us
    broadcast_in_dim x1, local copies, waits for them, and re-layouts, shards(): return jnp.transpose(out, (1, 0, 2))[None]  1.32 us

profile of v1, /device:TPU:25, one launch (start us, length us, event | category | flops | bytes accessed | tf_op | source)
XLA Modules:
  0.0 49.6 jit_solution(2817074244861229451)
XLA Ops:
  0.0 0.0 copy-start.4
  0.0 0.0 copy-start.1
  0.0 0.0 copy-start
  0.0 0.0 copy-start.3
  0.0 0.0 copy-start.2
  1.4 1.1 %copy.14 = f32[1,84,12,128]{3,1,2,0:T(8,128)S(1)} copy(f32[1,84,12,128]{3,0,2,1:T(1,128)} %param.9) | data formatting | bytes 1032192 | tf_op args[0]
  2.5 1.4 %copy.11.win_hbm = bf16[9,256,84]{2,1,0:T(8,128)(2,1)S(1)} copy(bf16[9,256,84]{1,2,0:T(8,128)(2,1)} %param.14) | data formatting | bytes 774144 | tf_op args[5]
  3.9 0.0 copy-done.4
  3.9 0.0 copy-done.1
  3.9 0.0 copy-done
  3.9 0.0 copy-done.3
  3.9 0.0 copy-done.2
  3.9 44.3 %shard_map.91 = f32[12,84,128]{2,1,0:T(8,128)S(1)} custom-call(f32[12,84,128]{2,1,0:T(8,128)S(1)} %bitcast.10, s32[1]{0:T(128)S(6)} %copy.15.steps_ref, s32[1]{0:T(128)S(6)} %copy.16.offset_ref, f32[1000]{0:T(1024)S(1)} %copy-done.2, f32[1000]{0:T(1024)S(1)} %copy-done.3, bf16[9,256,84]{2,1,0:T(8,128)(2,1)S(1)} %copy.11.win_hbm, ...), custom_call_target="tpu_custom_call" | custom-call | flops 6002049024 | bytes 4194304 | tf_op jit(solution)/shard_map/pallas_call | solution.py:293
  48.3 1.3 %copy.12 = f32[1,84,12,128]{3,0,2,1:T(1,128)} copy(f32[1,84,12,128]{3,1,2,0:T(8,128)S(1)} %bitcast.9) | data formatting | bytes 1032192 | tf_op jit(solution)/shard_map/broadcast_in_dim | solution.py:323
Async XLA Ops:
  0.0 3.9 %copy-start.4 = (f32[256]{0:T(256)S(1)}, f32[256]{0:T(256)}, u32[]{:S(2)}) copy-start(f32[256]{0:T(256)} %param.17) | copy-start | bytes 3076
  0.0 3.9 %copy-start.1 = (bf16[9,84,256]{2,1,0:T(8,128)(2,1)S(1)}, bf16[9,84,256]{2,1,0:T(8,128)(2,1)}, u32[]{:S(2)}) copy-start(bf16[9,84,256]{2,1,0:T(8,128)(2,1)} %wout_hbm.1) | copy-start | bytes 1161220
  0.0 3.9 %copy-start = (bf16[9,256,256]{2,1,0:T(8,128)(2,1)S(1)}, bf16[9,256,256]{2,1,0:T(8,128)(2,1)}, u32[]{:S(2)}) copy-start(bf16[9,256,256]{2,1,0:T(8,128)(2,1)} %wmid_hbm.1) | copy-start | bytes 3538948
  0.0 3.9 %copy-start.3 = (f32[1000]{0:T(1024)S(1)}, f32[1000]{0:T(1024)}, u32[]{:S(2)}) copy-start(f32[1000]{0:T(1024)} %ss_ref.1) | copy-start | bytes 12004
  0.0 3.9 %copy-start.2 = (f32[1000]{0:T(1024)S(1)}, f32[1000]{0:T(1024)}, u32[]{:S(2)}) copy-start(f32[1000]{0:T(1024)} %ls_ref.1) | copy-start | bytes 12004

commit v2 on v1

--- a/solution.py
+++ b/solution.py
@@ -8,6 +8,8 @@
 from jax.sharding import PartitionSpec as P
 
 SWEEPS = 2
+CHIP_LAG = 2
+CHAIN_LAG = 4
 MESH = pl.DeviceIdType.MESH
 
 
@@ -15,10 +17,10 @@
     return (value + multiple - 1) // multiple * multiple
 
 
-def kernel(dims, x_hbm, steps_ref, offset_ref, ls_ref, ss_ref, win_hbm, wmid_hbm, wout_hbm, emb_ref, out_ref,
-           win_v, wout_v, w1, w2, w3, eb, xf, xc, u1, u2, inc,
+def kernel(dims, x_hbm, steps_ref, offset_ref, ls_hbm, ss_hbm, win_hbm, wmid_hbm, wout_hbm, emb_ref, out_ref,
+           x_v, win_v, wout_v, w1, w2, w3, eb, xf, xc, u1, u2, inc,
            ra, rp, rs, re, rr, sf, sb, se, sr,
-           load_sem, wmid_sem, ssem, rsem):
+           ls_ref, ss_ref, load_sem, wmid_sem, small_sem, ssem, rsem):
     n, inner, F, CH, H, W, FP = dims
     outer = n // (2 * inner)
     K = H // 2
@@ -32,7 +34,7 @@
     a_next, a_prev = me + 2 * inner, me - 2 * inner
 
     loads = [
-        pltpu.make_async_copy(x_hbm, xf.at[pl.ds(1, H)], load_sem.at[0]),
+        pltpu.make_async_copy(x_hbm, x_v, load_sem.at[0]),
         pltpu.make_async_copy(win_hbm, win_v, load_sem.at[1]),
         pltpu.make_async_copy(wout_hbm, wout_v, load_sem.at[2]),
     ]
@@ -43,6 +45,14 @@
                 wmid_hbm.at[tap], w2.at[pl.ds(kb * CH, CH), pl.ds(ka * CH, CH)], wmid_sem.at[tap]
             )
         )
+    small = [
+        pltpu.make_async_copy(src, dst, small_sem.at[i])
+        for i, (src, dst) in enumerate(
+            ((ls_hbm, ls_ref), (ss_hbm, ss_ref))
+        )
+    ]
+    for copy in small:
+        copy.start()
     loads[1].start()
     loads[0].start()
     for copy in loads[2:]:
@@ -69,14 +79,6 @@
     for there, device in ((b > 0, b_prev), (b < inner - 1, b_next), (a > 0, a_prev), (a < outer - 1, a_next)):
         pl.when(there)(functools.partial(greet, device))
 
-    table_row = lax.rem(steps_ref[0] + offset_ref[0], ls_ref.shape[0])
-    log_noise = ls_ref[table_row]
-    step_len = ss_ref[table_row]
-    first = jnp.where(me == 0, 1.0, 0.0).astype(jnp.float32)
-
-    for block in range(CH // 128):
-        row = emb_ref[pl.ds(block, 1), :] * log_noise
-        eb[pl.ds(block * 128, 128), :] = jnp.transpose(jnp.broadcast_to(row, (128, 128)))
     zero_row = jnp.zeros((CH, W), jnp.bfloat16)
     for edge in (0, H + 1):
         u1[edge] = zero_row
@@ -86,9 +88,24 @@
     loads[1].wait()
     for kb in range(3):
         parts = [win_v[3 * ka + kb].astype(jnp.float32) for ka in range(3)]
-        parts.append(jnp.zeros((CH, w1.shape[1] - 3 * F), jnp.float32))
-        w1[pl.ds(kb * CH, CH), :] = jnp.concatenate(parts, axis=1).astype(jnp.bfloat16)
+        parts.append(jnp.zeros((w1.shape[1] - 3 * F, CH), jnp.float32))
+        stacked = jnp.concatenate(parts, axis=0)
+        w1[pl.ds(kb * CH, CH), :] = jnp.transpose(stacked).astype(jnp.bfloat16)
+    for copy in small:
+        copy.wait()
+    table = ls_ref.shape[1]
+    table_row = lax.rem(steps_ref[...] + offset_ref[...], jnp.full((1, 1), table, jnp.int32))
+    chosen = lax.broadcasted_iota(jnp.int32, (1, table), 1) == table_row
+    log_noise = jnp.sum(jnp.where(chosen, ls_ref[...], 0.0), axis=1, keepdims=True)
+    step_len = jnp.sum(jnp.where(chosen, ss_ref[...], 0.0), axis=1, keepdims=True)
+    first = jnp.where(me == 0, 1.0, 0.0).astype(jnp.float32)
+
+    for block in range(CH // 128):
+        row = emb_ref[pl.ds(block, 1), :] * log_noise
+        eb[pl.ds(block * 128, 128), :] = jnp.transpose(jnp.broadcast_to(row, (128, 128)))
     loads[0].wait()
+    for r in range(H):
+        xf[r + 1] = x_v[pl.ds(r, F, stride=H), :]
 
     lane = lax.broadcasted_iota(jnp.int32, (1, W), 1)
 
@@ -231,38 +248,71 @@
         result(s, k).wait_recv()
         finish(s, other(k), rr[s, k])
 
+    early = K - CHAIN_LAG
+
+    def compute(s, t):
+        if t < K:
+            conv1(t)
+        if s == 0 and t == 0:
+            for copy in loads[3:]:
+                copy.wait()
+        if 1 <= t <= K:
+            conv2(t - 1)
+        if s == 0 and t == 1:
+            loads[2].wait()
+            for tap in range(9):
+                ka, kb = tap // 3, tap % 3
+                padded = jnp.concatenate(
+                    [wout_v[tap].astype(jnp.float32), jnp.zeros((FP - F, CH), jnp.float32)], axis=0
+                )
+                w3[pl.ds(kb * FP, FP), pl.ds(ka * CH, CH)] = padded.astype(jnp.bfloat16)
+            count = 1 + (b > 0).astype(jnp.int32) + (b < inner - 1).astype(jnp.int32)
+            count = count + (a > 0).astype(jnp.int32) + (a < outer - 1).astype(jnp.int32)
+            pl.semaphore_wait(barrier, count)
+        if t >= 2:
+            conv3(s, t - 2)
+            send_pair(s, t - 2)
+            if t - 2 >= CHIP_LAG:
+                send_chip(s, t - 2 - CHIP_LAG)
+            if t - 2 >= CHAIN_LAG:
+                k = t - 2 - CHAIN_LAG
+                if s + 1 < SWEEPS:
+                    pl.when(a == 0)(lambda: send_plane(s, k))
+                else:
+                    send_plane(s, k)
+
     for s in range(SWEEPS):
         for t in range(K + 2):
-            if t < K:
-                conv1(t)
-            if s == 0 and t == 0:
-                for copy in loads[3:]:
-                    copy.wait()
-            if 1 <= t <= K:
-                conv2(t - 1)
-            if s == 0 and t == 1:
-                loads[2].wait()
-                for tap in range(9):
-                    ka, kb = tap // 3, tap % 3
-                    padded = jnp.concatenate(
-                        [wout_v[tap].astype(jnp.float32), jnp.zeros((FP - F, CH), jnp.float32)], axis=0
-                    )
-                    w3[pl.ds(kb * FP, FP), pl.ds(ka * CH, CH)] = padded.astype(jnp.bfloat16)
-                count = 1 + (b > 0).astype(jnp.int32) + (b < inner - 1).astype(jnp.int32)
-                count = count + (a > 0).astype(jnp.int32) + (a < outer - 1).astype(jnp.int32)
-                pl.semaphore_wait(barrier, count)
-            if t >= 2:
-                conv3(s, t - 2)
-                send_pair(s, t - 2)
-            if t >= 3:
-                send_chip(s, t - 3)
-            if t >= 4:
-                send_plane(s, t - 4)
-        send_chip(s, K - 1)
-        send_plane(s, K - 2)
-        send_plane(s, K - 1)
-        for k in range(K):
-            receive(s, k)
+            if s > 0:
+                if t == 0:
+                    receive(s - 1, 0)
+                    send_plane(s - 1, K - 3)
+                    receive(s - 1, 1)
+                else:
+                    if K - 3 + t < K:
+                        send_plane(s - 1, K - 3 + t)
+                    if t + 1 < K:
+                        receive(s - 1, t + 1)
+            compute(s, t)
+        for k in range(K - CHIP_LAG, K - 1):
+            send_chip(s, k)
+        last = s + 1 == SWEEPS
+        if last:
+            for k in range(early, K - 3):
+                send_plane(s, k)
+            send_chip(s, K - 1)
+            for k in range(K - 3, K):
+                send_plane(s, k)
+                if k - 2 >= 0:
+                    receive(s, k - 3)
+            for k in range(K - 3, K):
+                receive(s, k)
+        else:
+            for k in range(early, K - 3):
+                pl.when(a == 0)(lambda k=k: send_plane(s, k))
+            send_chip(s, K - 1)
+            for k in range(K - 3):
+                pl.when(a > 0)(lambda k=k: send_plane(s, k))
 
     for s in range(SWEEPS):
         for k in range(K):
@@ -283,9 +333,8 @@
     FP = up(F, 16)
     K1 = up(3 * F, 128)
     K = H // 2
-    x = jnp.transpose(states[0], (1, 0, 2))
+    x = states.reshape(F * H, W)
     vmem = pl.BlockSpec(memory_space=pltpu.VMEM)
-    smem = pl.BlockSpec(memory_space=pltpu.SMEM)
     hbm = pl.BlockSpec(memory_space=pl.ANY)
     bf16, f32 = jnp.bfloat16, jnp.float32
     slot = pltpu.VMEM((SWEEPS, K, F, W), f32)
@@ -293,10 +342,11 @@
     out = pl.pallas_call(
         functools.partial(kernel, (n, inner, F, CH, H, W, FP)),
         out_shape=jax.ShapeDtypeStruct((H, F, W), f32),
-        in_specs=[hbm, smem, smem, smem, smem, hbm, hbm, hbm, vmem],
+        in_specs=[hbm, vmem, vmem, hbm, hbm, hbm, hbm, hbm, vmem],
         out_specs=vmem,
         scratch_shapes=[
-            pltpu.VMEM(w_in.shape, bf16),
+            pltpu.VMEM((F * H, W), f32),
+            pltpu.VMEM((9, F, CH), bf16),
             pltpu.VMEM(w_out.shape, bf16),
             pltpu.VMEM((3 * CH, K1), bf16),
             pltpu.VMEM((3 * CH, 3 * CH), bf16),
@@ -308,18 +358,21 @@
             pltpu.VMEM((H + 2, CH, W), bf16),
             pltpu.VMEM((SWEEPS, H, F, W), f32),
             slot, slot, slot, slot, slot, slot, slot, slot, slot,
+            pltpu.VMEM((1, log_sigma.shape[0]), f32),
+            pltpu.VMEM((1, step_size.shape[0]), f32),
             pltpu.SemaphoreType.DMA((3,)),
             pltpu.SemaphoreType.DMA((9,)),
+            pltpu.SemaphoreType.DMA((2,)),
             pltpu.SemaphoreType.DMA((5, SWEEPS, K)),
             pltpu.SemaphoreType.DMA((5, SWEEPS, K)),
         ],
         compiler_params=pltpu.CompilerParams(
-            collective_id=0, has_side_effects=True, vmem_limit_bytes=40 * 1024 * 1024
+            collective_id=0, has_side_effects=True, vmem_limit_bytes=64 * 1024 * 1024
         ),
         cost_estimate=pl.CostEstimate(
             flops=flops, bytes_accessed=4 * 1024 * 1024, transcendentals=SWEEPS * 2 * CH * H * W
         ),
-    )(x, slab_steps, offset, log_sigma, step_size, w_in, w_mid, w_out, embed.reshape(CH // 128, 128))
+    )(x, slab_steps.reshape(1, 1), offset.reshape(1, 1), log_sigma.reshape(1, -1), step_size.reshape(1, -1), jnp.transpose(w_in, (0, 2, 1)), w_mid, w_out, embed.reshape(CH // 128, 128))
     return jnp.transpose(out, (1, 0, 2))[None]
 
 

time: 50 us -> 45 us (0.900)
  Pallas kernels: 44.3 us -> 41.1 us
  local copies, waits for them, and re-layouts: 3.77 us -> 2.36 us
    pallas_call x1, Pallas kernels: 44.3 us -> 41.1 us  [shards(): pl.pallas_call(functools.partial(kernel, (n, inner, F, CH, H, W, FP)), ou...]
    unnamed x12 -> x0, local copies, waits for them, and re-layouts: 2.45 us -> none
    broadcast_in_dim x1, local copies, waits for them, and re-layouts: 1.32 us -> 2.36 us  [shards(): return jnp.transpose(out, (1, 0, 2))[None]]
where the time goes in v2:
time: 45 us; the launch traced here: 44.8 us
  Pallas kernels  41.1 us (91%)
  local copies, waits for them, and re-layouts  2.36 us (5%)
  between operations  1.3 us (3%)
    pallas_call x1, Pallas kernels, shards(): pl.pallas_call(functools.partial(kernel, (n, inner, F, CH, H, W, FP)), ou...  41.1 us
    broadcast_in_dim x1, local copies, waits for them, and re-layouts, shards(): return jnp.transpose(out, (1, 0, 2))[None]  2.36 us

profile of v2, /device:TPU:25, one launch (start us, length us, event | category | flops | bytes accessed | tf_op | source)
XLA Modules:
  0.0 44.8 jit_solution(4158119803371528595)
XLA Ops:
  1.3 41.1 %shard_map.91 = f32[12,84,128]{2,1,0:T(8,128)} custom-call(f32[1008,128]{1,0:T(8,128)} %bitcast.13, s32[1,1]{1,0:T(1,128)} %bitcast.10.steps_ref, s32[1,1]{1,0:T(1,128)} %bitcast.11.offset_ref, f32[1,1000]{1,0:T(1,128)} %bitcast.15, f32[1,1000]{1,0:T(1,128)} %bitcast.16, bf16[9,84,256]{2,1,0:T(8,128)(2,1)} %bitcast.14, bf16[9,256,256]{2,1,0:T(8,128)(2,1)} %wmid_hbm.1, ...), custom_call_target="tpu_custom_call" | custom-call | flops 6002049024 | bytes 4194304 | tf_op jit(solution)/shard_map/pallas_call | solution.py:342
  42.4 2.4 %copy.10 = f32[1,84,12,128]{3,0,2,1:T(1,128)} copy(f32[1,84,12,128]{3,1,2,0:T(8,128)} %bitcast.12) | data formatting | bytes 1032192 | tf_op jit(solution)/shard_map/broadcast_in_dim | solution.py:376

commit v3 on v2

--- a/solution.py
+++ b/solution.py
@@ -8,7 +8,7 @@
 from jax.sharding import PartitionSpec as P
 
 SWEEPS = 2
-CHIP_LAG = 2
+CHIP_LAG = 1
 CHAIN_LAG = 4
 MESH = pl.DeviceIdType.MESH
 
@@ -18,7 +18,7 @@
 
 
 def kernel(dims, x_hbm, steps_ref, offset_ref, ls_hbm, ss_hbm, win_hbm, wmid_hbm, wout_hbm, emb_ref, out_ref,
-           x_v, win_v, wout_v, w1, w2, w3, eb, xf, xc, u1, u2, inc,
+           x_v, out_v, win_v, wout_v, w1, w2, w3, eb, xf, xc, u1, u2, inc,
            ra, rp, rs, re, rr, sf, sb, se, sr,
            ls_ref, ss_ref, load_sem, wmid_sem, small_sem, ssem, rsem):
     n, inner, F, CH, H, W, FP = dims
@@ -34,7 +34,7 @@
     a_next, a_prev = me + 2 * inner, me - 2 * inner
 
     loads = [
-        pltpu.make_async_copy(x_hbm, x_v, load_sem.at[0]),
+        pltpu.make_async_copy(x_hbm, x_v.at[pl.ds(0, F * H)], load_sem.at[0]),
         pltpu.make_async_copy(win_hbm, win_v, load_sem.at[1]),
         pltpu.make_async_copy(wout_hbm, wout_v, load_sem.at[2]),
     ]
@@ -242,7 +242,7 @@
         if s + 1 < SWEEPS:
             xf[r + 1] = before + first * xf[r + 1]
         else:
-            out_ref[r] = before + inc[s, r]
+            out_v[pl.ds(r, F, stride=H), :] = before + inc[s, r]
 
     def receive(s, k):
         result(s, k).wait_recv()
@@ -314,6 +314,8 @@
             for k in range(K - 3):
                 pl.when(a > 0)(lambda k=k: send_plane(s, k))
 
+    store = pltpu.make_async_copy(out_v.at[pl.ds(0, F * H)], out_ref, load_sem.at[3])
+    store.start()
     for s in range(SWEEPS):
         for k in range(K):
             pair(s, k).wait_send()
@@ -321,6 +323,7 @@
             pl.when(b > 0)(lambda s=s, k=k: backward(s, k).wait_send())
             pl.when(a < outer - 1)(lambda s=s, k=k: chain(s, k).wait_send())
             result(s, k).wait_send()
+    store.wait()
 
 
 def shards(n, states, slab_steps, offset, log_sigma, step_size, w_in, w_mid, w_out, embed):
@@ -341,11 +344,12 @@
     flops = SWEEPS * 2 * 9 * (2 * F * CH + CH * CH) * H * W
     out = pl.pallas_call(
         functools.partial(kernel, (n, inner, F, CH, H, W, FP)),
-        out_shape=jax.ShapeDtypeStruct((H, F, W), f32),
+        out_shape=jax.ShapeDtypeStruct((F * H, W), f32),
         in_specs=[hbm, vmem, vmem, hbm, hbm, hbm, hbm, hbm, vmem],
-        out_specs=vmem,
+        out_specs=hbm,
         scratch_shapes=[
-            pltpu.VMEM((F * H, W), f32),
+            pltpu.VMEM((up(F, 8) * H, W), f32),
+            pltpu.VMEM((up(F, 8) * H, W), f32),
             pltpu.VMEM((9, F, CH), bf16),
             pltpu.VMEM(w_out.shape, bf16),
             pltpu.VMEM((3 * CH, K1), bf16),
@@ -360,7 +364,7 @@
             slot, slot, slot, slot, slot, slot, slot, slot, slot,
             pltpu.VMEM((1, log_sigma.shape[0]), f32),
             pltpu.VMEM((1, step_size.shape[0]), f32),
-            pltpu.SemaphoreType.DMA((3,)),
+            pltpu.SemaphoreType.DMA((4,)),
             pltpu.SemaphoreType.DMA((9,)),
             pltpu.SemaphoreType.DMA((2,)),
             pltpu.SemaphoreType.DMA((5, SWEEPS, K)),
@@ -373,7 +377,7 @@
             flops=flops, bytes_accessed=4 * 1024 * 1024, transcendentals=SWEEPS * 2 * CH * H * W
         ),
     )(x, slab_steps.reshape(1, 1), offset.reshape(1, 1), log_sigma.reshape(1, -1), step_size.reshape(1, -1), jnp.transpose(w_in, (0, 2, 1)), w_mid, w_out, embed.reshape(CH // 128, 128))
-    return jnp.transpose(out, (1, 0, 2))[None]
+    return out.reshape(states.shape)
 
 
 def solution(mesh):

time: 45 us -> 42.2 us (0.938)
  Pallas kernels: 41.1 us -> 38.8 us
  local copies, waits for them, and re-layouts: 2.36 us -> 1.88 us
    broadcast_in_dim x1 -> x0, local copies, waits for them, and re-layouts: 2.36 us -> none  [shards(): return jnp.transpose(out, (1, 0, 2))[None]]
    pallas_call x1, Pallas kernels: 41.1 us -> 38.8 us  [shards(): pl.pallas_call(functools.partial(kernel, (n, inner, F, CH, H, W, FP)), ou...]
    unnamed x0 -> x1, local copies, waits for them, and re-layouts: none -> 1.88 us
where the time goes in v3:
time: 42.2 us; the launch traced here: 42 us
  Pallas kernels  38.8 us (92%)
  local copies, waits for them, and re-layouts  1.88 us (4%)
  between operations  1.3 us (3%)
    pallas_call x1, Pallas kernels, shards(): pl.pallas_call(functools.partial(kernel, (n, inner, F, CH, H, W, FP)), ou...  38.8 us
    unnamed x1, local copies, waits for them, and re-layouts  1.88 us

profile of v3, /device:TPU:25, one launch (start us, length us, event | category | flops | bytes accessed | tf_op | source)
XLA Modules:
  0.0 42.0 jit_solution(8869004806693912968)
XLA Ops:
  1.3 38.8 %shard_map.91 = f32[1008,128]{1,0:T(8,128)} custom-call(f32[1008,128]{1,0:T(8,128)} %bitcast.11, s32[1,1]{1,0:T(1,128)} %bitcast.8.steps_ref, s32[1,1]{1,0:T(1,128)} %bitcast.9.offset_ref, f32[1,1000]{1,0:T(1,128)} %bitcast.13, f32[1,1000]{1,0:T(1,128)} %bitcast.14, bf16[9,84,256]{2,1,0:T(8,128)(2,1)} %bitcast.12, bf16[9,256,256]{2,1,0:T(8,128)(2,1)} %wmid_hbm.1, ...), custom_call_target="tpu_custom_call" | custom-call | flops 6002049024 | bytes 4194304 | tf_op jit(solution)/shard_map/pallas_call | solution.py:345
  40.1 1.9 %copy.15 = f32[1,84,12,128]{3,0,2,1:T(1,128)} copy(f32[1,84,12,128]{3,0,2,1:T(1,128)} %bitcast.10) | data formatting | bytes 1032192
